TPU v7x, 32 devices: a whole 2x2x4 slice. The times are simulated.
32 devices in a mesh: dp: 4 (over y, x), seq: 8 (over z, core).
Axes of the slice: x: 2, y: 2, z: 4, core: 2. Of those that a mesh axis runs over, the one named last changes fastest.
Arguments:
- queries: bfloat16 [4, 3072, 4096], P('dp', 'seq'), may hold values from -0.59765625 to 0.59765625
- keys: bfloat16 [4, 3072, 4096], P('dp', 'seq'), may hold values from -0.59765625 to 0.59765625
- values: bfloat16 [4, 3072, 4096], P('dp', 'seq'), may hold values from -6 to 6
- grad_out: bfloat16 [4, 3072, 4096], P('dp', 'seq'), may hold values from -6 to 6
- gain: float32 [4096], replicated, may hold values from 0.1 to 1.9
Outputs:
- output: bfloat16 [4, 3072, 4096], P('dp', 'seq')
- grad_queries: bfloat16 [4, 3072, 4096], P('dp', 'seq')
- grad_keys: bfloat16 [4, 3072, 4096], P('dp', 'seq')
- grad_values: bfloat16 [4, 3072, 4096], P('dp', 'seq')
- grad_gain: float32 [4096], replicated
All inputs are finite; a program needn't handle non-finite values.
Results may differ from a plain program's by a relative error of at most 0.0051.
Values sent between devices are 32-bit elements; how exact they have to be, the bound alone decides.
A program may use at most 192 MiB of HBM per device.

v0:
```python
import jax
import jax.numpy as jnp
from jax import lax
from jax.sharding import PartitionSpec as P

H = 32
HD = 128


def carried_in(part, axis, combine, identity, reverse):
    count = lax.axis_size(axis)
    place = lax.axis_index(axis)
    ahead = count - 1 - place if reverse else place
    gathered = lax.all_gather(part, axis)
    state = jnp.zeros_like(part) + jnp.asarray(identity, part.dtype)

    def one(turn, state):
        source = count - 1 - turn if reverse else turn
        return combine(state, lax.dynamic_index_in_dim(gathered, source, 0, False))

    return lax.fori_loop(0, ahead, one, state)


def add_states(earlier, later):
    return earlier + later


def local(queries, keys, values, grad_out, gain):
    count = queries.shape[1]
    query = queries[0].reshape(count, H, HD)
    key_b = keys[0].reshape(count, H, HD)
    value = values[0].reshape(count, H, HD)
    row = lax.broadcasted_iota(jnp.int32, (count, count), 0)
    col = lax.broadcasted_iota(jnp.int32, (count, count), 1)
    mask = (row >= col)[None]
    high = lax.Precision.HIGHEST
    zero = jnp.zeros((H, HD, HD), jnp.float32)
    block_state = jnp.einsum("thd,the->hde", key_b, value, preferred_element_type=jnp.float32)
    prefix = carried_in(block_state, "seq", add_states, zero, False)
    scores = jnp.einsum("thd,ihd->hti", query, key_b, preferred_element_type=jnp.float32)
    probs = jnp.where(mask, scores, 0.0).astype(jnp.bfloat16)
    attn = jnp.einsum("hti,ihe->the", probs, value, preferred_element_type=jnp.float32)
    attn = attn + jnp.einsum("thd,hde->the", query.astype(jnp.float32), prefix, precision=high)
    flat = attn.reshape(count, H * HD)
    rms = jnp.sqrt(jnp.mean(flat * flat, axis=-1, keepdims=True) + 1e-05)
    normed = flat / rms
    output = (normed * gain).astype(jnp.bfloat16)
    upstream = grad_out[0].astype(jnp.float32)
    gain_term = jnp.sum(upstream * normed, axis=0)
    grad_gain = lax.psum(lax.psum(gain_term, "seq"), "dp")
    g_normed = upstream * gain
    d_flat = (
        (g_normed - normed * jnp.mean(g_normed * normed, axis=-1, keepdims=True)) / rms
    ).astype(jnp.bfloat16)
    d_attn = d_flat.reshape(count, H, HD)
    block_grad = jnp.einsum("thd,the->hde", query, d_attn, preferred_element_type=jnp.float32)
    suffix = carried_in(block_grad, "seq", add_states, zero, True)
    earlier = carried_in(block_state, "seq", add_states, zero, False)
    dscores = jnp.einsum("the,ihe->hti", d_attn, value, preferred_element_type=jnp.float32)
    dprobs = jnp.where(mask, dscores, 0.0).astype(jnp.bfloat16)
    grad_q = jnp.einsum("hti,ihd->thd", dprobs, key_b, preferred_element_type=jnp.float32)
    grad_q = grad_q + jnp.einsum(
        "the,hde->thd", d_attn.astype(jnp.float32), earlier, precision=high
    )
    grad_k = jnp.einsum("hti,thd->ihd", dprobs, query, preferred_element_type=jnp.float32)
    grad_k = grad_k + jnp.einsum("ihe,hde->ihd", value.astype(jnp.float32), suffix, precision=high)
    grad_v = jnp.einsum("hti,the->ihe", probs, d_attn, preferred_element_type=jnp.float32)
    grad_v = grad_v + jnp.einsum("ihd,hde->ihe", key_b.astype(jnp.float32), suffix, precision=high)
    shape_out = (1, count, H * HD)
    return (
        output.reshape(shape_out),
        grad_q.astype(jnp.bfloat16).reshape(shape_out),
        grad_k.astype(jnp.bfloat16).reshape(shape_out),
        grad_v.astype(jnp.bfloat16).reshape(shape_out),
        grad_gain,
    )


def solution(mesh):
    in_specs = (
        P("dp", "seq", None),
        P("dp", "seq", None),
        P("dp", "seq", None),
        P("dp", "seq", None),
        P(),
    )
    out_specs = (
        P("dp", "seq", None),
        P("dp", "seq", None),
        P("dp", "seq", None),
        P("dp", "seq", None),
        P(),
    )
    return jax.shard_map(local, mesh=mesh, in_specs=in_specs, out_specs=out_specs, check_vma=False)
```

profile of v0, /device:TPU:1, one launch (start us, length us, event | category | flops | bytes accessed | tf_op | source)
XLA Modules:
  0.0 438.1 jit_solution(3570706818431418171)
XLA Ops:
  7.2 0.0 all-gather.5.cloned.1.call-start
  7.2 4.4 %copy.61 = bf16[48,8,32,128]{3,2,1,0:T(8,128)(2,1)} copy(bf16[48,8,32,128]{3,1,2,0:T(8,128)(2,1)} %bitcast.88) | data formatting | bytes 6291456
  11.6 3.8 copy.36
  15.4 0.0 copy-start.7
  15.4 3.9 copy.62
  19.3 0.0 copy-start.3
  19.3 0.0 copy-done.7
  19.3 1.6 copy-done.3
  20.9 3.8 fusion.12
  24.7 0.0 all-gather.5.cloned.1.call-update
  24.7 0.6 all-gather.7.cloned.1.call-start
  25.3 2.7 copy.60
  28.0 0.0 copy-start
  28.0 6.0 %copy.41 = f32[1,384,4096]{1,2,0:T(8,128)} copy(bf16[1,384,4096]{2,1,0:T(8,128)(2,1)} %param.12) | data formatting | bytes 9437184 | tf_op jit(solution)/shard_map/convert_element_type | solution.py:48
  34.0 0.0 copy-done
  34.1 13.8 %select_convert_fusion.1 = bf16[32,384,384]{2,1,0:T(8,128)(2,1)} fusion(pred[384,384]{1,0:T(8,128)(4,1)S(1)} %iota_compare_fusion, bf16[384,32,128]{2,1,0:T(8,128)(2,1)} %bitcast.80, bf16[384,32,128]{2,1,0:T(8,128)(2,1)S(1)} %bitcast.71), kind=kOutput, calls=%fused_computation.3 | convolution fusion | flops 1217396736 | bytes 15876096 | tf_op jit(solution)/shard_map/thd,ihd->hti/dot_general | solution.py:40
  47.8 11.4 %fusion.8 = f32[32,384,128]{1,2,0:T(8,128)} fusion(bf16[32,384,384]{2,1,0:T(8,128)(2,1)} %select_convert_fusion.1, bf16[384,32,128]{2,1,0:T(8,128)(2,1)} %bitcast.76), kind=kOutput, calls=%fused_computation.22 | convolution fusion | flops 1207959552 | bytes 18874368 | tf_op jit(solution)/shard_map/hti,ihe->the/dot_general | solution.py:42
  59.3 119.2 %all-gather.5.cloned.1.call-done = f32[256,128,128]{2,1,0:T(8,128)} async-done(((f32[32,128,128]{2,1,0:T(8,128)}), f32[256,128,128]{2,1,0:T(8,128)}) %all-gather.5.cloned.1.call-update) | async-done | bytes 16777232 | tf_op jit(solution)/shard_map/all_gather | solution.py:14
  178.5 0.2 broadcast_in_dim.28.clone
  178.7 2.3 while.26
  178.7 2.1 bitcast_add_fusion.7
  181.1 12.3 %multiply_reduce_fusion = (f32[384]{0:T(512)S(1)}, f32[384,32,128]{0,2,1:T(8,128)}) fusion(f32[32,128,128]{2,1,0:T(8,128)S(1)} %get-tuple-element.92, bf16[384,32,128]{2,1,0:T(8,128)(2,1)} %bitcast.72, f32[32,384,128]{1,2,0:T(8,128)} %fusion.8), kind=kOutput, calls=%fused_computation.17 | convolution fusion | flops 2420637184 | bytes 17827328 | tf_op jit(solution)/shard_map/thd,hde->the/dot_general | solution.py:43
  193.4 0.0 copy-start.8
  193.4 6.6 %copy.42 = f32[384,4096]{1,0:T(8,128)} copy(f32[384,4096]{0,1:T(8,128)} %bitcast.69) | data formatting | bytes 12582912 | tf_op jit(solution)/shard_map/reshape | solution.py:44
  200.0 0.0 copy-done.8
  200.0 4.7 %fusion.4 = (f32[4096]{0:T(1024)S(1)}, f32[384]{0:T(512)S(1)}) fusion(bf16[1,384,4096]{2,1,0:T(8,128)(2,1)} %param.12, f32[384,4096]{1,0:T(8,128)} %copy.42, f32[384]{0:T(512)S(1)} %add_sqrt_fusion, f32[4096]{0:T(1024)S(1)} %copy-done.8), kind=kLoop, calls=%fused_computation.12 | loop fusion | flops 11005568 | bytes 9473024 | tf_op jit(solution)/shard_map/reduce_sum | solution.py:49
  204.7 0.0 copy-start.1
  204.7 5.5 %divide_convert_fusion = bf16[384,32,128]{0,2,1:T(8,128)(2,1)S(1)} fusion(f32[384,32,128]{0,2,1:T(8,128)} %get-tuple-element.127, f32[384,32,128]{0,2,1:T(8,128)} %bitcast.82, f32[384]{0:T(512)S(1)} %broadcast_multiply_fusion, f32[384]{0:T(512)S(1)} %add_sqrt_fusion, f32[32,128]{1,0:T(8,128)S(1)} %bitcast.91), kind=kLoop, calls=%fused_computation.15 | loop fusion | flops 9437184 | bytes 15748096 | tf_op jit(solution)/shard_map/convert_element_type | solution.py:54
  210.2 0.0 copy-start.4
  210.2 1.7 copy-done.4
  211.9 0.0 copy-done.1
  212.0 3.8 fusion.20
  215.7 2.9 copy.49
  218.6 0.0 all-gather.7.cloned.1.call-update
  218.6 6.8 %copy.40 = f32[1,384,4096]{2,1,0:T(8,128)} copy(f32[1,384,4096]{1,2,0:T(8,128)} %bitcast.70) | data formatting | bytes 12582912 | tf_op jit(solution)/shard_map/reshape | solution.py:44
  225.4 11.9 %select_convert_fusion = bf16[32,384,384]{2,1,0:T(8,128)(2,1)} fusion(pred[384,384]{1,0:T(8,128)(4,1)S(1)} %iota_compare_fusion, bf16[384,32,128]{0,2,1:T(8,128)(2,1)} %copy-done.4, bf16[384,32,128]{2,1,0:T(8,128)(2,1)} %bitcast.77), kind=kOutput, calls=%fused_computation.2 | convolution fusion | flops 1217396736 | bytes 15876096 | tf_op jit(solution)/shard_map/the,ihe->hti/dot_general | solution.py:59
  237.3 0.0 copy-start.5
  237.3 12.4 %fusion.23 = f32[32,384,128]{1,2,0:T(8,128)} fusion(bf16[32,384,384]{2,1,0:T(8,128)(2,1)} %select_convert_fusion, bf16[384,32,128]{0,2,1:T(8,128)(2,1)} %copy-done.7), kind=kOutput, calls=%fused_computation.38 | convolution fusion | flops 1207959552 | bytes 18874368 | tf_op jit(solution)/shard_map/hti,ihd->thd/dot_general | solution.py:61
  249.7 0.0 copy-done.5
  249.7 6.3 %fusion.1 = bf16[384,32,128]{0,2,1:T(8,128)(2,1)} fusion(f32[32,384,128]{1,2,0:T(8,128)} %fusion.23, f32[32,128,128]{2,1,0:T(8,128)S(1)} %get-tuple-element.92, bf16[384,32,128]{0,2,1:T(8,128)(2,1)S(1)} %copy-done.5), kind=kOutput, calls=%fused_computation.7 | convolution fusion | flops 2419064832 | bytes 14680064 | tf_op jit(solution)/shard_map/the,hde->thd/dot_general | solution.py:62
  256.0 0.0 copy-start.2
  256.0 4.8 %copy.53 = bf16[1,384,4096]{2,1,0:T(8,128)(2,1)} copy(bf16[1,384,4096]{1,2,0:T(8,128)(2,1)} %bitcast.84) | data formatting | bytes 6291456
  260.8 34.3 %psum.14 = f32[4096]{0:T(1024)S(1)} all-reduce(f32[4096]{0:T(1024)S(1)} %get-tuple-element.108), channel_id=1, replica_groups=mesh['dp'=4,'seq'=8] {'seq'}, use_global_device_ids=true, to_apply=%region_7.8 | all-reduce | flops 4096 | bytes 32768 | tf_op jit(solution)/shard_map/psum | solution.py:50
  295.1 15.1 %psum.15 = f32[4096]{0:T(1024)} all-reduce(f32[4096]{0:T(1024)S(1)} %psum.14), channel_id=1, replica_groups=mesh['dp'=4,'seq'=8] {'dp'}, use_global_device_ids=true, to_apply=%region_8.9 | all-reduce | flops 4096 | bytes 32768 | tf_op jit(solution)/shard_map/psum | solution.py:50
  310.2 0.0 copy-done.2
  310.2 9.9 %fusion.14 = f32[32,384,128]{1,2,0:T(8,128)} fusion(bf16[32,384,384]{2,1,0:T(8,128)(2,1)} %select_convert_fusion, bf16[384,32,128]{2,1,0:T(8,128)(2,1)S(1)} %bitcast.74), kind=kOutput, calls=%fused_computation.28 | convolution fusion | flops 1207959552 | bytes 18874368 | tf_op jit(solution)/shard_map/hti,thd->ihd/dot_general | solution.py:65
  320.2 5.4 %multiply_convert_fusion = bf16[1,384,4096]{2,1,0:T(8,128)(2,1)} fusion(f32[1,384,4096]{2,1,0:T(8,128)} %copy.40, f32[4096]{0:T(1024)S(1)} %copy-done.8, f32[384]{0:T(512)S(1)} %add_sqrt_fusion), kind=kLoop, calls=%fused_computation.16 | loop fusion | flops 4718592 | bytes 9455104 | tf_op jit(solution)/shard_map/convert_element_type | solution.py:47
  325.6 55.8 %all-gather.7.cloned.1.call-done = f32[256,128,128]{2,1,0:T(8,128)} async-done(((f32[32,128,128]{2,1,0:T(8,128)}), f32[256,128,128]{2,1,0:T(8,128)}) %all-gather.7.cloned.1.call-update) | async-done | bytes 16777232 | tf_op jit(solution)/shard_map/all_gather | solution.py:14
  381.4 0.2 broadcast_in_dim.28
  381.6 12.9 %while.27 = (s32[]{:T(128)}, f32[32,128,128]{2,1,0:T(8,128)S(1)}, s32[]{:T(128)}, f32[8,32,128,128]{3,2,1,0:T(8,128)}, s32[]{:T(128)}, /*index=5*/s32[]{:T(128)}, s32[]{:T(128)}, s32[]{:T(128)}) while((s32[]{:T(128)}, f32[32,128,128]{2,1,0:T(8,128)S(1)}, s32[]{:T(128)}, f32[8,32,128,128]{3,2,1,0:T(8,128)}, s32[]{:T(128)}, ...), condition=%wide.region_5.6_spmd, body=%wide.region_4.5_spmd.sunk | while | flops 524294 | bytes 6291599 | solution.py:21
  381.6 2.1 bitcast_add_fusion.8
  383.8 2.1 bitcast_add_fusion.8
  385.9 2.1 bitcast_add_fusion.8
  388.1 2.1 bitcast_add_fusion.8
  390.3 2.1 bitcast_add_fusion.8
  392.4 2.1 bitcast_add_fusion.8
  394.5 0.0 copy-start.6
  394.6 8.0 %fusion.5 = f32[32,128,384]{2,1,0:T(8,128)S(1)} fusion(f32[32,128,128]{2,1,0:T(8,128)S(1)} %get-tuple-element.93, bf16[384,32,128]{2,1,0:T(8,128)(2,1)} %bitcast.81), kind=kOutput, calls=%fused_computation.19 | convolution fusion | flops 2415919104 | bytes 11534336 | tf_op jit(solution)/shard_map/ihd,hde->ihe/dot_general | solution.py:68
  402.5 0.0 copy-done.6
  402.5 7.9 %add_convert_fusion = bf16[32,128,384]{2,1,0:T(8,128)(2,1)} fusion(f32[32,128,384]{2,1,0:T(8,128)S(1)} %fusion.5, bf16[384,32,128]{0,2,1:T(8,128)(2,1)S(1)} %copy-done.6, bf16[32,384,384]{2,1,0:T(8,128)(2,1)} %select_convert_fusion.1), kind=kOutput, calls=%fused_computation.14 | convolution fusion | flops 1211105280 | bytes 22020096 | tf_op jit(solution)/shard_map/hti,the->ihe/dot_general | solution.py:67
  410.4 4.8 %copy.55 = bf16[1,384,4096]{2,1,0:T(8,128)(2,1)} copy(bf16[1,384,4096]{1,2,0:T(8,128)(2,1)} %bitcast.85) | data formatting | bytes 6291456
  415.2 11.3 %fusion = bf16[384,32,128]{0,2,1:T(8,128)(2,1)} fusion(f32[32,384,128]{1,2,0:T(8,128)} %fusion.14, f32[32,128,128]{2,1,0:T(8,128)S(1)} %get-tuple-element.93, bf16[384,32,128]{2,1,0:T(8,128)(2,1)} %bitcast.78), kind=kOutput, calls=%fused_computation.5 | convolution fusion | flops 2419064832 | bytes 14680064 | tf_op jit(solution)/shard_map/ihe,hde->ihd/dot_general | solution.py:66
  426.4 4.6 %copy.54 = bf16[1,384,4096]{2,1,0:T(8,128)(2,1)} copy(bf16[1,384,4096]{1,2,0:T(8,128)(2,1)} %bitcast.83) | data formatting | bytes 6291456
  (3 shorter events, 0.1 us)
Async XLA Ops:
  7.2 171.3 %all-gather.5.cloned.1.call-start = ((), (), s32[]{:S(2)}) async-start(), calls=%async_computation | async-start | bytes 18874368 | tf_op jit(solution)/shard_map/all_gather | solution.py:14
  15.4 3.9 copy-start.7
  19.3 1.6 copy-start.3
  24.7 356.7 %all-gather.7.cloned.1.call-start = ((), (), s32[]{:S(2)}) async-start(), calls=%async_computation.1 | async-start | bytes 18874368 | tf_op jit(solution)/shard_map/all_gather | solution.py:14
  28.0 6.0 %copy-start = (bf16[48,8,32,128]{3,2,1,0:T(8,128)(2,1)}, bf16[48,8,32,128]{3,2,1,0:T(8,128)(2,1)S(1)}, u32[]{:S(2)}) copy-start(bf16[48,8,32,128]{3,2,1,0:T(8,128)(2,1)S(1)} %copy.60) | copy-start | bytes 9437188
  193.4 6.6 %copy-start.8 = (f32[4096]{0:T(1024)S(1)}, f32[4096]{0:T(1024)}, u32[]{:S(2)}) copy-start(f32[4096]{0:T(1024)} %param.13) | copy-start | bytes 49156
  204.7 7.2 %copy-start.1 = (bf16[48,8,32,128]{3,2,1,0:T(8,128)(2,1)S(1)}, bf16[48,8,32,128]{3,2,1,0:T(8,128)(2,1)}, u32[]{:S(2)}) copy-start(bf16[48,8,32,128]{3,2,1,0:T(8,128)(2,1)} %copy-done) | copy-start | bytes 9437188
  210.2 1.7 copy-start.4
  237.3 12.4 %copy-start.5 = (bf16[384,32,128]{0,2,1:T(8,128)(2,1)S(1)}, bf16[384,32,128]{0,2,1:T(8,128)(2,1)}, u32[]{:S(2)}) copy-start(bf16[384,32,128]{0,2,1:T(8,128)(2,1)} %copy-done.4) | copy-start | bytes 9437188
  256.0 54.2 %copy-start.2 = (bf16[48,8,32,128]{3,2,1,0:T(8,128)(2,1)S(1)}, bf16[48,8,32,128]{3,2,1,0:T(8,128)(2,1)}, u32[]{:S(2)}) copy-start(bf16[48,8,32,128]{3,2,1,0:T(8,128)(2,1)} %copy-done) | copy-start | bytes 9437188
  394.5 8.0 %copy-start.6 = (bf16[384,32,128]{0,2,1:T(8,128)(2,1)S(1)}, bf16[384,32,128]{0,2,1:T(8,128)(2,1)}, u32[]{:S(2)}) copy-start(bf16[384,32,128]{0,2,1:T(8,128)(2,1)} %copy-done.4) | copy-start | bytes 9437188
Sparse Core Ops, SparseCore 0:
  24.8 153.6 all-gather.4
  218.7 162.5 all-gather.6
where the time goes:
time: 445 us; the launch traced here: 438 us
  waiting for transfers between devices  175 us (39%)
  matrix products  113 us (25%)
  local copies, waits for them, and re-layouts  55 us (12%)
  blocking collectives  49.4 us (11%)
  other arithmetic  30.6 us (7%)
  between operations  14.4 us (3%)
    all_gather x2, waiting for transfers between devices, carried_in(): gathered = lax.all_gather(part, axis)  175 us
    psum x2, blocking collectives, local(): grad_gain = lax.psum(lax.psum(gain_term, 'seq'), 'dp')  49.4 us
    unnamed x24, local copies, waits for them, and re-layouts  28.6 us
    add x7, other arithmetic, add_states(): return earlier + later  14.9 us
    dot_general x1, matrix products, local(): jnp.einsum('thd,ihd->hti', query, key_b, preferred_element_type=jnp.float32)  13.8 us
    reshape x2, local copies, waits for them, and re-layouts, local(): flat = attn.reshape(count, H * HD)  13.3 us
    dot_general x1, matrix products, local(): jnp.einsum('hti,ihd->thd', dprobs, key_b, preferred_element_type=jnp.floa...  12.4 us
    dot_general x1, matrix products, local(): jnp.einsum('thd,hde->the', query.astype(jnp.float32), prefix, precision=h...  12.3 us
  transfers between devices with their start and end apart: 2, of which 2 were waited for; matrix products, arithmetic and copies ran while one was open for 21% of the time, Pallas kernels for 0%

commit v1 on v0

v1 whole, which is shorter than its diff:
```python
import functools

import jax
import jax.numpy as jnp
from jax import lax
from jax.experimental import pallas as pl
from jax.experimental.pallas import tpu as pltpu
from jax.sharding import PartitionSpec as P

HD = 128
F32 = jnp.float32
BF16 = jnp.bfloat16


def dot(a, b, ca, cb):
    return lax.dot_general(a, b, (((ca,), (cb,)), ((), ())), preferred_element_type=F32)


def split(x):
    hi = x.astype(BF16)
    return hi, (x - hi.astype(F32)).astype(BF16)


def twice(x):
    return jnp.concatenate([x, x], axis=1)


def times_state(x, state):
    hi, lo = split(state)
    return dot(twice(x), jnp.concatenate([hi, lo], axis=0), 1, 0)


def times_state_t(x, state):
    hi, lo = split(state)
    return dot(twice(x), jnp.concatenate([hi, lo], axis=1), 1, 1)


def kernel(
    S, D, T, H,
    q_hbm, k_hbm, v_hbm, g_hbm, gain,
    out_hbm, gq_hbm, gk_hbm, gv_hbm, gg,
    q, k, v, g, acc1, acc2, ob, gqb, gkb, gvb,
    st, base1, psd1, pst1, car1, pcar1, base2, psd2, pst2, car2, pcar2, pre,
    ssq, gdot, gt, gp, dpb, sqb,
    in_sem, out_sem, gk_sem, gv_sem, sems1, sems2, pair_sem, dp_sem, sq_sem,
):
    C = S // 2
    half = H // 2
    inner = H * HD
    s = lax.axis_index("seq")
    d = lax.axis_index("dp")
    c = lax.div(s, 2)
    core = lax.rem(s, 2)
    partner = s + 1 - 2 * core

    def cols(h):
        return pl.ds(pl.multiple_of(h * HD, HD), HD)

    def mine(i):
        return core * half + i

    def other(i):
        return (1 - core) * half + i

    def remote(src, dst, send, recv, axis, peer):
        return pltpu.make_async_remote_copy(
            src_ref=src, dst_ref=dst, send_sem=send, recv_sem=recv,
            device_id={axis: peer}, device_id_type=pl.DeviceIdType.MESH,
        )

    loads = [
        pltpu.make_async_copy(src.at[0], dst, in_sem.at[n])
        for n, (src, dst) in enumerate(((k_hbm, k), (v_hbm, v), (q_hbm, q), (g_hbm, g)))
    ]
    for load in loads:
        load.start()

    barrier = pltpu.get_barrier_semaphore()
    greet = [("seq", partner)]
    greet += [("seq", lax.rem(s + 2 * j, S)) for j in range(1, C)]
    greet += [("dp", lax.rem(d + j, D)) for j in range(1, D)]
    for axis, peer in greet:
        pl.semaphore_signal(
            barrier, inc=1, device_id={axis: peer}, device_id_type=pl.DeviceIdType.MESH
        )
    ssq[...] = jnp.zeros_like(ssq)
    gdot[...] = jnp.zeros_like(gdot)

    @pl.when(c == 0)
    def _():
        car1[...] = jnp.zeros_like(car1)

    @pl.when(c == C - 1)
    def _():
        car2[...] = jnp.zeros_like(car2)

    row = lax.broadcasted_iota(jnp.int32, (T, T), 0)
    col = lax.broadcasted_iota(jnp.int32, (T, T), 1)

    class Scan:
        def __init__(self, forward, base, psd, pst, car, pcar, sems):
            self.base, self.psd, self.pst, self.car, self.pcar = base, psd, pst, car, pcar
            self.sems = sems
            step = 2 if forward else -2
            self.next = lax.rem(s + step + S, S)
            self.first = (c == 0) if forward else (c == C - 1)
            self.last = (c == C - 1) if forward else (c == 0)
            self.lead = (core == 0) if forward else (core == 1)

        def state_copy(self, i):
            return remote(st.at[other(i)], self.pst.at[i], self.sems.at[0, i], self.sems.at[1, i], "seq", partner)

        def carry_copy(self, i):
            return remote(self.base.at[i], self.car.at[i], self.sems.at[2, i], self.sems.at[3, i], "seq", self.next)

        def share_copy(self, i):
            return remote(self.psd.at[i], self.pcar.at[i], self.sems.at[4, i], self.sems.at[5, i], "seq", partner)

        def begin(self, i):
            self.state_copy(i).wait_recv()
            self.base[i] = st[mine(i)] + self.pst[i]

            @pl.when(self.first)
            def _():
                self.carry_copy(i).start()

        def step(self, i):
            @pl.when(jnp.logical_not(self.first))
            def _():
                self.carry_copy(i).wait_recv()

            @pl.when(jnp.logical_not(jnp.logical_or(self.first, self.last)))
            def _():
                self.base[i] = self.base[i] + self.car[i]
                self.carry_copy(i).start()

            came = self.car[i]

            @pl.when(self.lead)
            def _():
                self.psd[i] = came + st[mine(i)]

            @pl.when(jnp.logical_not(self.lead))
            def _():
                self.psd[i] = came

            self.share_copy(i).start()
            return jnp.where(self.lead, came, came + self.pst[i])

        def shared(self, i):
            self.share_copy(i).wait_recv()
            return self.pcar[i]

        def drain_states(self):
            @pl.loop(0, half)
            def _(i):
                self.state_copy(i).wait_send()

        def drain(self):
            @pl.loop(0, half)
            def _(i):
                self.share_copy(i).wait_send()

            @pl.when(jnp.logical_not(self.last))
            def _():
                @pl.loop(0, half)
                def _(i):
                    self.carry_copy(i).wait_send()

    up = Scan(True, base1, psd1, pst1, car1, pcar1, sems1)
    down = Scan(False, base2, psd2, pst2, car2, pcar2, sems2)

    loads[0].wait()
    loads[1].wait()
    pl.semaphore_wait(barrier, len(greet))

    @pl.loop(0, half)
    def _(i):
        for h in (other(i), mine(i)):
            st[h] = dot(k[:, cols(h)], v[:, cols(h)], 0, 0)
        up.state_copy(i).start()

        @pl.when(i >= 1)
        def _():
            up.begin(i - 1)

    up.begin(half - 1)
    loads[2].wait()
    loads[3].wait()

    def inter(h, prefix):
        pre[h] = prefix
        a = acc1[:, cols(h)] + times_state(q[:, cols(h)], prefix)
        acc1[:, cols(h)] = a
        ssq[...] += a * a
        gdot[...] += g[:, cols(h)].astype(F32) * gain[pl.ds(h, 1), :] * a

    @pl.loop(0, half)
    def _(i):
        for h in (mine(i), other(i)):
            scores = dot(q[:, cols(h)], k[:, cols(h)], 1, 1)
            probs = jnp.where(row >= col, scores, 0.0).astype(BF16)
            acc1[:, cols(h)] = dot(probs, v[:, cols(h)], 1, 0)
        inter(mine(i), up.step(i))

        @pl.when(i >= 1)
        def _():
            inter(other(i - 1), up.shared(i - 1))

    inter(other(half - 1), up.shared(half - 1))
    up.drain_states()

    inv = lax.rsqrt(jnp.sum(ssq[...], axis=1, keepdims=True) * (1.0 / inner) + 1e-05)
    mean = jnp.sum(gdot[...], axis=1, keepdims=True) * inv * (1.0 / inner)
    ssq[...] = jnp.broadcast_to(inv, (T, HD))
    gdot[...] = jnp.broadcast_to(mean, (T, HD))

    @pl.loop(0, half)
    def _(i):
        for h in (other(i), mine(i)):
            scale = gain[pl.ds(h, 1), :]
            normed = acc1[:, cols(h)] * ssq[...]
            ob[:, cols(h)] = (normed * scale).astype(BF16)
            upstream = g[:, cols(h)].astype(F32)
            gt[pl.ds(h, 1), :] = jnp.sum(upstream * normed, axis=0, keepdims=True)
            d_attn = ((upstream * scale - normed * gdot[...]) * ssq[...]).astype(BF16)
            g[:, cols(h)] = d_attn
            st[h] = dot(q[:, cols(h)], d_attn, 0, 0)
        down.state_copy(i).start()

        @pl.when(i >= 1)
        def _():
            down.begin(i - 1)

    down.begin(half - 1)
    pair = remote(gt, gp, pair_sem.at[0], pair_sem.at[1], "seq", partner)
    pair.start()
    write_out = pltpu.make_async_copy(ob, out_hbm.at[0], out_sem.at[0])
    write_out.start()
    write_gq = pltpu.make_async_copy(gqb, gq_hbm.at[0], out_sem.at[1])

    def dp_copy(j):
        return remote(dpb.at[d], dpb.at[d], dp_sem.at[0, j], dp_sem.at[1, j], "dp", lax.rem(d + j, D))

    def sq_copy(j):
        return remote(sqb.at[c], sqb.at[c], sq_sem.at[0, j], sq_sem.at[1, j], "seq", lax.rem(s + 2 * j, S))

    def out_copies(h):
        return (
            pltpu.make_async_copy(gkb.at[:, cols(h)], gk_hbm.at[0, :, cols(h)], gk_sem.at[h]),
            pltpu.make_async_copy(gvb.at[:, cols(h)], gv_hbm.at[0, :, cols(h)], gv_sem.at[h]),
        )

    def finish(h, suffix):
        gkb[:, cols(h)] = (acc1[:, cols(h)] + times_state_t(v[:, cols(h)], suffix)).astype(BF16)
        gvb[:, cols(h)] = (acc2[:, cols(h)] + times_state(k[:, cols(h)], suffix)).astype(BF16)
        for copy in out_copies(h):
            copy.start()

    @pl.loop(0, half)
    def _(i):
        for h in (mine(i), other(i)):
            qh, kh, vh, dh = (x[:, cols(h)] for x in (q, k, v, g))
            probs_t = jnp.where(row <= col, dot(kh, qh, 1, 1), 0.0).astype(BF16)
            acc2[:, cols(h)] = dot(probs_t, dh, 1, 0)
            d_probs_t = jnp.where(row <= col, dot(vh, dh, 1, 1), 0.0).astype(BF16)
            acc1[:, cols(h)] = dot(d_probs_t, qh, 1, 0)
            d_probs = jnp.where(row >= col, dot(dh, vh, 1, 1), 0.0).astype(BF16)
            grad_q = dot(d_probs, kh, 1, 0) + times_state_t(dh, pre[h])
            gqb[:, cols(h)] = grad_q.astype(BF16)

        finish(mine(i), down.step(i))

        @pl.when(i >= 1)
        def _():
            finish(other(i - 1), down.shared(i - 1))

        @pl.when(i == half // 4)
        def _():
            pair.wait()
            dpb[d] = gt[...] + gp[...]
            for j in range(1, D):
                dp_copy(j).start()

        @pl.when(i == half // 2)
        def _():
            for j in range(1, D):
                dp_copy(j).wait()
            total = dpb[0]
            for j in range(1, D):
                total = total + dpb[j]
            sqb[c] = total
            for j in range(1, C):
                sq_copy(j).start()

    write_gq.start()
    finish(other(half - 1), down.shared(half - 1))
    for j in range(1, C):
        sq_copy(j).wait()
    total = sqb[0]
    for j in range(1, C):
        total = total + sqb[j]
    gg[...] = total
    up.drain()
    down.drain_states()
    down.drain()
    write_out.wait()
    write_gq.wait()

    @pl.loop(0, H)
    def _(h):
        for copy in out_copies(h):
            copy.wait()


def local(S, D, queries, keys, values, grad_out, gain):
    _, T, inner = queries.shape
    H = inner // HD
    half = H // 2
    big = jax.ShapeDtypeStruct((1, T, inner), BF16)
    anyspec = pl.BlockSpec(memory_space=pl.ANY)
    vmem = pl.BlockSpec(memory_space=pltpu.VMEM)
    wide16 = pltpu.VMEM((T, inner), BF16)
    wide32 = pltpu.VMEM((T, inner), F32)
    part = pltpu.VMEM((half, HD, HD), F32)
    whole = pltpu.VMEM((H, HD, HD), F32)
    row = pltpu.VMEM((H, HD), F32)
    sem = pltpu.SemaphoreType.DMA
    flops = 2 * T * HD * inner * 26
    out = pl.pallas_call(
        functools.partial(kernel, S, D, T, H),
        out_shape=(big, big, big, big, jax.ShapeDtypeStruct((H, HD), F32)),
        in_specs=[anyspec] * 4 + [vmem],
        out_specs=(anyspec,) * 4 + (vmem,),
        scratch_shapes=[wide16] * 4 + [wide32] * 2 + [wide16] * 4
        + [whole] + [part] * 10 + [whole]
        + [pltpu.VMEM((T, HD), F32)] * 2
        + [row, row, pltpu.VMEM((D, H, HD), F32), pltpu.VMEM((S // 2, H, HD), F32)]
        + [sem((4,)), sem((2,)), sem((H,)), sem((H,)), sem((6, half)), sem((6, half)),
           sem((2,)), sem((2, D)), sem((2, S // 2))],
        compiler_params=pltpu.CompilerParams(
            collective_id=0, has_side_effects=True, vmem_limit_bytes=60 * 1024 * 1024
        ),
        cost_estimate=pl.CostEstimate(
            flops=flops, bytes_accessed=8 * T * inner * 2, transcendentals=0
        ),
    )(queries, keys, values, grad_out, gain.reshape(H, HD))
    return out[:4] + (out[4].reshape(inner),)


def solution(mesh):
    wide = P("dp", "seq", None)
    return jax.shard_map(
        functools.partial(local, mesh.shape["seq"], mesh.shape["dp"]),
        mesh=mesh,
        in_specs=(wide, wide, wide, wide, P()),
        out_specs=(wide, wide, wide, wide, P()),
        check_vma=False,
    )
```

time: 445 us -> 116 us (0.26); the launches traced: 438 us -> 115 us
  waiting for transfers between devices: 175 us -> 0 us
  matrix products: 113 us -> 0 us
  Pallas kernels: 0 us -> 102 us
  blocking collectives: 49.4 us -> 0 us
  local copies, waits for them, and re-layouts: 55 us -> 12.4 us
  other arithmetic: 30.6 us -> 0 us
  between operations: 14.4 us -> 0.65 us
    all_gather x2 -> x0, waiting for transfers between devices: 175 us -> none  [carried_in(): gathered = lax.all_gather(part, axis)]
    dot_general x12 -> x0, matrix products: 113 us -> none  [the longest x1 13.8 us: local(): jnp.einsum('thd,ihd->hti', query, key_b, preferred_element_type=jnp.float32)]
    pallas_call x0 -> x1, Pallas kernels: none -> 102 us  [local(): pl.pallas_call(functools.partial(kernel, S, D, T, H), out_shape=(big, big...]
    psum x2 -> x0, blocking collectives: 49.4 us -> none  [local(): grad_gain = lax.psum(lax.psum(gain_term, 'seq'), 'dp')]
    unnamed x24 -> x13, local copies, waits for them, and re-layouts: 28.6 us -> 12.4 us
    add x7 -> x0, other arithmetic: 14.9 us -> none  [add_states(): return earlier + later]
    reshape x2 -> x0, local copies, waits for them, and re-layouts: 13.3 us -> none  [local(): flat = attn.reshape(count, H * HD)]
    convert_element_type x2 -> x0, other arithmetic: 10.9 us -> none  [the longest x1 5.46 us: local(): d_flat = ((g_normed - normed * jnp.mean(g_normed * normed, axis=-1, keepd...]
  transfers between devices with their start and end apart: 2 -> 0, of which waited for: 2 -> 0; matrix products, arithmetic and copies ran while one was open for 21% -> 0% of each run, Pallas kernels for 0% -> 0%
where the time goes in v1:
time: 116 us; the launch traced here: 115 us
  Pallas kernels  102 us (88%)
  local copies, waits for them, and re-layouts  12.4 us (11%)
    pallas_call x1, Pallas kernels, local(): pl.pallas_call(functools.partial(kernel, S, D, T, H), out_shape=(big, big...  102 us
    unnamed x13, local copies, waits for them, and re-layouts  12.4 us

profile of v1, /device:TPU:1, one launch (start us, length us, event | category | flops | bytes accessed | tf_op | source)
XLA Modules:
  0.0 115.1 jit_solution(6060279742091449087)
XLA Ops:
  0.6 102.0 %shard_map.92 = (bf16[1,384,4096]{2,1,0:T(8,128)(2,1)}, bf16[1,384,4096]{2,1,0:T(8,128)(2,1)}, bf16[1,384,4096]{2,1,0:T(8,128)(2,1)}, bf16[1,384,4096]{2,1,0:T(8,128)(2,1)}, f32[32,128]{1,0:T(8,128)}) custom-call(bf16[1,384,4096]{2,1,0:T(8,128)(2,1)} %q_hbm.1, bf16[1,384,4096]{2,1,0:T(8,128)(2,1)} %k_hbm.1, bf16[1,384,4096]{2,1,0:T(8,128)(2,1)} %v_hbm.1, ...), custom_call_target="tpu_custom_call" | custom-call | flops 10468982784 | bytes 25165824 | tf_op jit(solution)/shard_map/pallas_call | solution.py:330
  102.7 0.0 copy-start.2
  102.7 4.1 %copy.15 = bf16[1,384,4096]{2,1,0:T(8,128)(2,1)} copy(bf16[1,384,4096]{2,1,0:T(8,128)(2,1)} %get-tuple-element.20) | data formatting | bytes 6291456
  106.7 0.0 copy-done.2
  106.7 0.0 copy-start.1
  106.7 1.7 %copy.16 = bf16[1,384,4096]{2,1,0:T(8,128)(2,1)} copy(bf16[1,384,4096]{2,1,0:T(8,128)(2,1)S(1)} %copy-done.2) | data formatting | bytes 6291456
  108.4 1.4 %copy-done.1 = bf16[1,384,4096]{2,1,0:T(8,128)(2,1)S(1)} copy-done((bf16[1,384,4096]{2,1,0:T(8,128)(2,1)S(1)}, bf16[1,384,4096]{2,1,0:T(8,128)(2,1)}, u32[]{:S(2)}) %copy-start.1) | copy-done | bytes 3145752
  109.8 0.0 copy-start
  109.8 1.7 %copy.17 = bf16[1,384,4096]{2,1,0:T(8,128)(2,1)} copy(bf16[1,384,4096]{2,1,0:T(8,128)(2,1)S(1)} %copy-done.1) | data formatting | bytes 6291456
  111.4 1.4 %copy-done = bf16[1,384,4096]{2,1,0:T(8,128)(2,1)S(1)} copy-done((bf16[1,384,4096]{2,1,0:T(8,128)(2,1)S(1)}, bf16[1,384,4096]{2,1,0:T(8,128)(2,1)}, u32[]{:S(2)}) %copy-start) | copy-done | bytes 3145752
  112.8 0.0 copy-start.3
  112.8 1.7 %copy.18 = bf16[1,384,4096]{2,1,0:T(8,128)(2,1)} copy(bf16[1,384,4096]{2,1,0:T(8,128)(2,1)S(1)} %copy-done) | data formatting | bytes 6291456
  114.5 0.0 copy-done.3
  114.5 0.6 copy.19
Async XLA Ops:
  102.7 4.1 %copy-start.2 = (bf16[1,384,4096]{2,1,0:T(8,128)(2,1)S(1)}, bf16[1,384,4096]{2,1,0:T(8,128)(2,1)}, u32[]{:S(2)}) copy-start(bf16[1,384,4096]{2,1,0:T(8,128)(2,1)} %get-tuple-element.21) | copy-start | bytes 9437188
  106.7 3.0 %copy-start.1 = (bf16[1,384,4096]{2,1,0:T(8,128)(2,1)S(1)}, bf16[1,384,4096]{2,1,0:T(8,128)(2,1)}, u32[]{:S(2)}) copy-start(bf16[1,384,4096]{2,1,0:T(8,128)(2,1)} %get-tuple-element.22) | copy-start | bytes 9437188
  109.8 3.0 %copy-start = (bf16[1,384,4096]{2,1,0:T(8,128)(2,1)S(1)}, bf16[1,384,4096]{2,1,0:T(8,128)(2,1)}, u32[]{:S(2)}) copy-start(bf16[1,384,4096]{2,1,0:T(8,128)(2,1)} %get-tuple-element.23) | copy-start | bytes 9437188
  112.8 1.7 %copy-start.3 = (f32[32,128]{1,0:T(8,128)S(1)}, f32[32,128]{1,0:T(8,128)}, u32[]{:S(2)}) copy-start(f32[32,128]{1,0:T(8,128)} %get-tuple-element.14) | copy-start | bytes 49156

commit v2 on v1

--- a/solution.py
+++ b/solution.py
@@ -38,11 +38,11 @@
 def kernel(
     S, D, T, H,
     q_hbm, k_hbm, v_hbm, g_hbm, gain,
-    out_hbm, gq_hbm, gk_hbm, gv_hbm, gg,
-    q, k, v, g, acc1, acc2, ob, gqb, gkb, gvb,
+    ob, gqb, gkb, gvb, gg,
+    q, k, v, g, acc1, acc2,
     st, base1, psd1, pst1, car1, pcar1, base2, psd2, pst2, car2, pcar2, pre,
     ssq, gdot, gt, gp, dpb, sqb,
-    in_sem, out_sem, gk_sem, gv_sem, sems1, sems2, pair_sem, dp_sem, sq_sem,
+    in_sem, sems1, sems2, pair_sem, dp_sem, sq_sem,
 ):
     C = S // 2
     half = H // 2
@@ -94,8 +94,19 @@
     def _():
         car2[...] = jnp.zeros_like(car2)
 
-    row = lax.broadcasted_iota(jnp.int32, (T, T), 0)
-    col = lax.broadcasted_iota(jnp.int32, (T, T), 1)
+    cut = 2 * HD if T > 2 * HD else T
+    later = [(0, cut)] + ([(cut, T)] if cut < T else [])
+    early = ([(0, T - cut)] if cut < T else []) + [(T - cut, T)]
+
+    def masked(x, at):
+        row = lax.broadcasted_iota(jnp.int32, x.shape, 0) + at
+        col = lax.broadcasted_iota(jnp.int32, x.shape, 1)
+        return jnp.where(row >= col, x, 0.0).astype(BF16)
+
+    def masked_t(x):
+        row = lax.broadcasted_iota(jnp.int32, x.shape, 0)
+        col = lax.broadcasted_iota(jnp.int32, x.shape, 1)
+        return jnp.where(row <= col, x, 0.0).astype(BF16)
 
     class Scan:
         def __init__(self, forward, base, psd, pst, car, pcar, sems):
@@ -198,9 +209,9 @@
     @pl.loop(0, half)
     def _(i):
         for h in (mine(i), other(i)):
-            scores = dot(q[:, cols(h)], k[:, cols(h)], 1, 1)
-            probs = jnp.where(row >= col, scores, 0.0).astype(BF16)
-            acc1[:, cols(h)] = dot(probs, v[:, cols(h)], 1, 0)
+            for lo, hi in later:
+                probs = masked(dot(q[lo:hi, cols(h)], k[:hi, cols(h)], 1, 1), lo)
+                acc1[lo:hi, cols(h)] = dot(probs, v[:hi, cols(h)], 1, 0)
         inter(mine(i), up.step(i))
 
         @pl.when(i >= 1)
@@ -235,39 +246,30 @@
     down.begin(half - 1)
     pair = remote(gt, gp, pair_sem.at[0], pair_sem.at[1], "seq", partner)
     pair.start()
-    write_out = pltpu.make_async_copy(ob, out_hbm.at[0], out_sem.at[0])
-    write_out.start()
-    write_gq = pltpu.make_async_copy(gqb, gq_hbm.at[0], out_sem.at[1])
 
     def dp_copy(j):
         return remote(dpb.at[d], dpb.at[d], dp_sem.at[0, j], dp_sem.at[1, j], "dp", lax.rem(d + j, D))
 
     def sq_copy(j):
         return remote(sqb.at[c], sqb.at[c], sq_sem.at[0, j], sq_sem.at[1, j], "seq", lax.rem(s + 2 * j, S))
-
-    def out_copies(h):
-        return (
-            pltpu.make_async_copy(gkb.at[:, cols(h)], gk_hbm.at[0, :, cols(h)], gk_sem.at[h]),
-            pltpu.make_async_copy(gvb.at[:, cols(h)], gv_hbm.at[0, :, cols(h)], gv_sem.at[h]),
-        )
 
     def finish(h, suffix):
         gkb[:, cols(h)] = (acc1[:, cols(h)] + times_state_t(v[:, cols(h)], suffix)).astype(BF16)
         gvb[:, cols(h)] = (acc2[:, cols(h)] + times_state(k[:, cols(h)], suffix)).astype(BF16)
-        for copy in out_copies(h):
-            copy.start()
 
     @pl.loop(0, half)
     def _(i):
         for h in (mine(i), other(i)):
-            qh, kh, vh, dh = (x[:, cols(h)] for x in (q, k, v, g))
-            probs_t = jnp.where(row <= col, dot(kh, qh, 1, 1), 0.0).astype(BF16)
-            acc2[:, cols(h)] = dot(probs_t, dh, 1, 0)
-            d_probs_t = jnp.where(row <= col, dot(vh, dh, 1, 1), 0.0).astype(BF16)
-            acc1[:, cols(h)] = dot(d_probs_t, qh, 1, 0)
-            d_probs = jnp.where(row >= col, dot(dh, vh, 1, 1), 0.0).astype(BF16)
-            grad_q = dot(d_probs, kh, 1, 0) + times_state_t(dh, pre[h])
-            gqb[:, cols(h)] = grad_q.astype(BF16)
+            at = cols(h)
+            for lo, hi in early:
+                probs_t = masked_t(dot(k[lo:hi, at], q[lo:, at], 1, 1))
+                acc2[lo:hi, at] = dot(probs_t, g[lo:, at], 1, 0)
+                d_probs_t = masked_t(dot(v[lo:hi, at], g[lo:, at], 1, 1))
+                acc1[lo:hi, at] = dot(d_probs_t, q[lo:, at], 1, 0)
+            for lo, hi in later:
+                d_probs = masked(dot(g[lo:hi, at], v[:hi, at], 1, 1), lo)
+                grad_q = dot(d_probs, k[:hi, at], 1, 0) + times_state_t(g[lo:hi, at], pre[h])
+                gqb[lo:hi, at] = grad_q.astype(BF16)
 
         finish(mine(i), down.step(i))
 
@@ -293,7 +295,6 @@
             for j in range(1, C):
                 sq_copy(j).start()
 
-    write_gq.start()
     finish(other(half - 1), down.shared(half - 1))
     for j in range(1, C):
         sq_copy(j).wait()
@@ -304,19 +305,23 @@
     up.drain()
     down.drain_states()
     down.drain()
-    write_out.wait()
-    write_gq.wait()
-
-    @pl.loop(0, H)
-    def _(h):
-        for copy in out_copies(h):
-            copy.wait()
+
+
+def write(*refs):
+    done = refs[10]
+    pairs = [(refs[n], refs[5 + n].at[0]) for n in range(4)] + [(refs[4], refs[9])]
+    copies = [pltpu.make_async_copy(src, dst, done.at[n]) for n, (src, dst) in enumerate(pairs)]
+    for copy in copies:
+        copy.start()
+    for copy in copies:
+        copy.wait()
 
 
 def local(S, D, queries, keys, values, grad_out, gain):
     _, T, inner = queries.shape
     H = inner // HD
     half = H // 2
+    held = pltpu.VMEM((T, inner), BF16)
     big = jax.ShapeDtypeStruct((1, T, inner), BF16)
     anyspec = pl.BlockSpec(memory_space=pl.ANY)
     vmem = pl.BlockSpec(memory_space=pltpu.VMEM)
@@ -329,23 +334,31 @@
     flops = 2 * T * HD * inner * 26
     out = pl.pallas_call(
         functools.partial(kernel, S, D, T, H),
-        out_shape=(big, big, big, big, jax.ShapeDtypeStruct((H, HD), F32)),
+        out_shape=(held, held, held, held, pltpu.VMEM((H, HD), F32)),
         in_specs=[anyspec] * 4 + [vmem],
-        out_specs=(anyspec,) * 4 + (vmem,),
-        scratch_shapes=[wide16] * 4 + [wide32] * 2 + [wide16] * 4
+        out_specs=(vmem,) * 5,
+        scratch_shapes=[wide16] * 4 + [wide32] * 2
         + [whole] + [part] * 10 + [whole]
         + [pltpu.VMEM((T, HD), F32)] * 2
         + [row, row, pltpu.VMEM((D, H, HD), F32), pltpu.VMEM((S // 2, H, HD), F32)]
-        + [sem((4,)), sem((2,)), sem((H,)), sem((H,)), sem((6, half)), sem((6, half)),
+        + [sem((4,)), sem((6, half)), sem((6, half)),
            sem((2,)), sem((2, D)), sem((2, S // 2))],
         compiler_params=pltpu.CompilerParams(
-            collective_id=0, has_side_effects=True, vmem_limit_bytes=60 * 1024 * 1024
+            collective_id=0, has_side_effects=True, vmem_limit_bytes=46 * 1024 * 1024
         ),
         cost_estimate=pl.CostEstimate(
             flops=flops, bytes_accessed=8 * T * inner * 2, transcendentals=0
         ),
     )(queries, keys, values, grad_out, gain.reshape(H, HD))
-    return out[:4] + (out[4].reshape(inner),)
+    wide = pl.pallas_call(
+        write,
+        out_shape=(big,) * 4 + (jax.ShapeDtypeStruct((H, HD), F32),),
+        in_specs=[anyspec] * 5,
+        out_specs=(anyspec,) * 5,
+        scratch_shapes=[sem((5,))],
+        cost_estimate=pl.CostEstimate(flops=0, bytes_accessed=8 * T * inner, transcendentals=0),
+    )(*out)
+    return tuple(wide[:4]) + (wide[4].reshape(inner),)
 
 
 def solution(mesh):

time: 116 us -> 496 us (4.28)
  Pallas kernels: 102 us -> 488 us
  local copies, waits for them, and re-layouts: 12.4 us -> 7.28 us
    pallas_call x1 -> x2, Pallas kernels: 102 us -> 488 us  [the longest x1 383 us: local(): pl.pallas_call(write, out_shape=(big,) * 4 + (jax.ShapeDtypeStruct((H, HD...]
    unnamed x13 -> x10, local copies, waits for them, and re-layouts: 12.4 us -> 7.28 us
where the time goes in v2:
time: 496 us
  Pallas kernels  488 us (98%)
  local copies, waits for them, and re-layouts  7.28 us (1%)
    pallas_call x1, Pallas kernels, local(): pl.pallas_call(write, out_shape=(big,) * 4 + (jax.ShapeDtypeStruct((H, HD...  383 us
    pallas_call x1, Pallas kernels, local(): pl.pallas_call(functools.partial(kernel, S, D, T, H), out_shape=(held, he...  105 us

profile of v2, /device:TPU:1, one launch (start us, length us, event | category | flops | bytes accessed | tf_op | source)
XLA Modules:
  0.0 495.6 jit_solution(14330415104472618461)
XLA Ops:
  0.6 104.8 %shard_map.92 = (bf16[384,4096]{1,0:T(8,128)(2,1)S(1)}, bf16[384,4096]{1,0:T(8,128)(2,1)S(1)}, bf16[384,4096]{1,0:T(8,128)(2,1)S(1)}, bf16[384,4096]{1,0:T(8,128)(2,1)S(1)}, f32[32,128]{1,0:T(8,128)S(1)}) custom-call(bf16[1,384,4096]{2,1,0:T(8,128)(2,1)} %q_hbm.1, bf16[1,384,4096]{2,1,0:T(8,128)(2,1)} %k_hbm.1, bf16[1,384,4096]{2,1,0:T(8,128)(2,1)} %v_hbm.1, ...), custom_call_target="tpu_custom_call" | custom-call | flops 10468982784 | bytes 25165824 | tf_op jit(solution)/shard_map/pallas_call | solution.py:335
  105.5 0.0 copy-start
  105.5 1.6 copy-done
  107.1 0.0 copy-start.1
  107.1 1.7 copy-done.1
  108.8 0.0 copy-start.2
  108.8 1.7 copy-done.2
  110.5 0.0 copy-start.3
  110.5 1.7 copy-done.3
  112.1 0.0 copy-start.4
  112.1 0.6 copy-done.4
  112.7 382.8 %shard_map.93 = (bf16[1,384,4096]{2,1,0:T(8,128)(2,1)}, bf16[1,384,4096]{2,1,0:T(8,128)(2,1)}, bf16[1,384,4096]{2,1,0:T(8,128)(2,1)}, bf16[1,384,4096]{2,1,0:T(8,128)(2,1)}, f32[32,128]{1,0:T(8,128)}) custom-call(bf16[384,4096]{1,0:T(8,128)(2,1)} %copy-done, bf16[384,4096]{1,0:T(8,128)(2,1)} %copy-done.1, bf16[384,4096]{1,0:T(8,128)(2,1)} %copy-done.2, ...), custom_call_target="tpu_custom_call" | custom-call | bytes 12582912 | tf_op jit(solution)/shard_map/pallas_call | solution.py:353
Async XLA Ops:
  105.5 1.7 copy-start
  107.1 1.7 copy-start.1
  108.8 1.7 copy-start.2
  110.5 1.7 copy-start.3
  112.1 0.6 copy-start.4

commit v3 on v2

--- a/solution.py
+++ b/solution.py
@@ -40,7 +40,7 @@
     q_hbm, k_hbm, v_hbm, g_hbm, gain,
     ob, gqb, gkb, gvb, gg,
     q, k, v, g, acc1, acc2,
-    st, base1, psd1, pst1, car1, pcar1, base2, psd2, pst2, car2, pcar2, pre,
+    st, base, psd, pst1, car1, pcar1, pst2, car2, pcar2, pre, q_t, probs_a, probs_b,
     ssq, gdot, gt, gp, dpb, sqb,
     in_sem, sems1, sems2, pair_sem, dp_sem, sq_sem,
 ):
@@ -94,9 +94,9 @@
     def _():
         car2[...] = jnp.zeros_like(car2)
 
-    cut = 2 * HD if T > 2 * HD else T
-    later = [(0, cut)] + ([(cut, T)] if cut < T else [])
-    early = ([(0, T - cut)] if cut < T else []) + [(T - cut, T)]
+    cut = probs_b.shape[1]
+    later = [(0, cut), (cut, T)]
+    early = [(0, T - cut), (T - cut, T)]
 
     def masked(x, at):
         row = lax.broadcasted_iota(jnp.int32, x.shape, 0) + at
@@ -178,8 +178,8 @@
                 def _(i):
                     self.carry_copy(i).wait_send()
 
-    up = Scan(True, base1, psd1, pst1, car1, pcar1, sems1)
-    down = Scan(False, base2, psd2, pst2, car2, pcar2, sems2)
+    up = Scan(True, base, psd, pst1, car1, pcar1, sems1)
+    down = Scan(False, base, psd, pst2, car2, pcar2, sems2)
 
     loads[0].wait()
     loads[1].wait()
@@ -212,6 +212,9 @@
             for lo, hi in later:
                 probs = masked(dot(q[lo:hi, cols(h)], k[:hi, cols(h)], 1, 1), lo)
                 acc1[lo:hi, cols(h)] = dot(probs, v[:hi, cols(h)], 1, 0)
+            for held, (lo, hi) in zip((probs_a, probs_b), early):
+                held[h] = masked_t(dot(k[lo:hi, cols(h)], q[lo:, cols(h)], 1, 1))
+            q_t[h] = q[:, cols(h)].T
         inter(mine(i), up.step(i))
 
         @pl.when(i >= 1)
@@ -220,6 +223,7 @@
 
     inter(other(half - 1), up.shared(half - 1))
     up.drain_states()
+    up.drain()
 
     inv = lax.rsqrt(jnp.sum(ssq[...], axis=1, keepdims=True) * (1.0 / inner) + 1e-05)
     mean = jnp.sum(gdot[...], axis=1, keepdims=True) * inv * (1.0 / inner)
@@ -236,7 +240,7 @@
             gt[pl.ds(h, 1), :] = jnp.sum(upstream * normed, axis=0, keepdims=True)
             d_attn = ((upstream * scale - normed * gdot[...]) * ssq[...]).astype(BF16)
             g[:, cols(h)] = d_attn
-            st[h] = dot(q[:, cols(h)], d_attn, 0, 0)
+            st[h] = dot(q_t[h], d_attn, 1, 0)
         down.state_copy(i).start()
 
         @pl.when(i >= 1)
@@ -261,9 +265,8 @@
     def _(i):
         for h in (mine(i), other(i)):
             at = cols(h)
-            for lo, hi in early:
-                probs_t = masked_t(dot(k[lo:hi, at], q[lo:, at], 1, 1))
-                acc2[lo:hi, at] = dot(probs_t, g[lo:, at], 1, 0)
+            for held, (lo, hi) in zip((probs_a, probs_b), early):
+                acc2[lo:hi, at] = dot(held[h], g[lo:, at], 1, 0)
                 d_probs_t = masked_t(dot(v[lo:hi, at], g[lo:, at], 1, 1))
                 acc1[lo:hi, at] = dot(d_probs_t, q[lo:, at], 1, 0)
             for lo, hi in later:
@@ -302,7 +305,6 @@
     for j in range(1, C):
         total = total + sqb[j]
     gg[...] = total
-    up.drain()
     down.drain_states()
     down.drain()
 
@@ -321,6 +323,7 @@
     _, T, inner = queries.shape
     H = inner // HD
     half = H // 2
+    cut = 2 * HD
     held = pltpu.VMEM((T, inner), BF16)
     big = jax.ShapeDtypeStruct((1, T, inner), BF16)
     anyspec = pl.BlockSpec(memory_space=pl.ANY)
@@ -338,13 +341,14 @@
         in_specs=[anyspec] * 4 + [vmem],
         out_specs=(vmem,) * 5,
         scratch_shapes=[wide16] * 4 + [wide32] * 2
-        + [whole] + [part] * 10 + [whole]
+        + [whole] + [part] * 8 + [whole]
+        + [pltpu.VMEM((H, HD, T), BF16), pltpu.VMEM((H, T - cut, T), BF16), pltpu.VMEM((H, cut, cut), BF16)]
         + [pltpu.VMEM((T, HD), F32)] * 2
         + [row, row, pltpu.VMEM((D, H, HD), F32), pltpu.VMEM((S // 2, H, HD), F32)]
         + [sem((4,)), sem((6, half)), sem((6, half)),
            sem((2,)), sem((2, D)), sem((2, S // 2))],
         compiler_params=pltpu.CompilerParams(
-            collective_id=0, has_side_effects=True, vmem_limit_bytes=46 * 1024 * 1024
+            collective_id=0, has_side_effects=True, vmem_limit_bytes=49 * 1024 * 1024
         ),
         cost_estimate=pl.CostEstimate(
             flops=flops, bytes_accessed=8 * T * inner * 2, transcendentals=0
@@ -353,10 +357,11 @@
     wide = pl.pallas_call(
         write,
         out_shape=(big,) * 4 + (jax.ShapeDtypeStruct((H, HD), F32),),
-        in_specs=[anyspec] * 5,
+        in_specs=[vmem] * 5,
         out_specs=(anyspec,) * 5,
         scratch_shapes=[sem((5,))],
         cost_estimate=pl.CostEstimate(flops=0, bytes_accessed=8 * T * inner, transcendentals=0),
+        compiler_params=pltpu.CompilerParams(vmem_limit_bytes=16 * 1024 * 1024),
     )(*out)
     return tuple(wide[:4]) + (wide[4].reshape(inner),)
 

time: 496 us -> 101 us (0.20)
  Pallas kernels: 488 us -> 101 us
  local copies, waits for them, and re-layouts: 7.28 us -> 0 us
    pallas_call x1, Pallas kernels: 383 us -> 4.73 us  [local(): pl.pallas_call(write, out_shape=(big,) * 4 + (jax.ShapeDtypeStruct((H, HD...]
    pallas_call x1, Pallas kernels: 105 us -> 95.9 us  [local(): pl.pallas_call(functools.partial(kernel, S, D, T, H), out_shape=(held, he...]
    unnamed x10 -> x0, local copies, waits for them, and re-layouts: 7.28 us -> none
where the time goes in v3:
time: 101 us
  Pallas kernels  101 us (100%)
    pallas_call x1, Pallas kernels, local(): pl.pallas_call(functools.partial(kernel, S, D, T, H), out_shape=(held, he...  95.9 us
    pallas_call x1, Pallas kernels, local(): pl.pallas_call(write, out_shape=(big,) * 4 + (jax.ShapeDtypeStruct((H, HD...  4.73 us

profile of v3, /device:TPU:1, one launch (start us, length us, event | category | flops | bytes accessed | tf_op | source)
XLA Modules:
  0.0 101.3 jit_solution(13929947857941388040)
XLA Ops:
  0.6 95.9 %shard_map.92 = (bf16[384,4096]{1,0:T(8,128)(2,1)S(1)}, bf16[384,4096]{1,0:T(8,128)(2,1)S(1)}, bf16[384,4096]{1,0:T(8,128)(2,1)S(1)}, bf16[384,4096]{1,0:T(8,128)(2,1)S(1)}, f32[32,128]{1,0:T(8,128)S(1)}) custom-call(bf16[1,384,4096]{2,1,0:T(8,128)(2,1)} %q_hbm.1, bf16[1,384,4096]{2,1,0:T(8,128)(2,1)} %k_hbm.1, bf16[1,384,4096]{2,1,0:T(8,128)(2,1)} %v_hbm.1, ...), custom_call_target="tpu_custom_call" | custom-call | flops 10468982784 | bytes 25165824 | tf_op jit(solution)/shard_map/pallas_call | solution.py:338
  96.5 4.7 %shard_map.93 = (bf16[1,384,4096]{2,1,0:T(8,128)(2,1)}, bf16[1,384,4096]{2,1,0:T(8,128)(2,1)}, bf16[1,384,4096]{2,1,0:T(8,128)(2,1)}, bf16[1,384,4096]{2,1,0:T(8,128)(2,1)}, f32[32,128]{1,0:T(8,128)}) custom-call(bf16[384,4096]{1,0:T(8,128)(2,1)S(1)} %get-tuple-element.15.refs_0_, bf16[384,4096]{1,0:T(8,128)(2,1)S(1)} %get-tuple-element.16.refs_1_, ...), custom_call_target="tpu_custom_call" | custom-call | bytes 12582912 | tf_op jit(solution)/shard_map/pallas_call | solution.py:357

commit v4 on v3

--- a/solution.py
+++ b/solution.py
@@ -206,8 +206,11 @@
         ssq[...] += a * a
         gdot[...] += g[:, cols(h)].astype(F32) * gain[pl.ds(h, 1), :] * a
 
-    @pl.loop(0, half)
-    def _(i):
+    ahead_up = half * c // (2 * C)
+    gap = C - 1 - c
+    ahead_down = half * gap * gap * gap // (C - 1) ** 3
+
+    def forward_blocks(i):
         for h in (mine(i), other(i)):
             for lo, hi in later:
                 probs = masked(dot(q[lo:hi, cols(h)], k[:hi, cols(h)], 1, 1), lo)
@@ -215,6 +218,17 @@
             for held, (lo, hi) in zip((probs_a, probs_b), early):
                 held[h] = masked_t(dot(k[lo:hi, cols(h)], q[lo:, cols(h)], 1, 1))
             q_t[h] = q[:, cols(h)].T
+
+    @pl.loop(0, ahead_up)
+    def _(i):
+        forward_blocks(i)
+
+    @pl.loop(0, half)
+    def _(i):
+        @pl.when(i + ahead_up < half)
+        def _():
+            forward_blocks(i + ahead_up)
+
         inter(mine(i), up.step(i))
 
         @pl.when(i >= 1)
@@ -261,8 +275,7 @@
         gkb[:, cols(h)] = (acc1[:, cols(h)] + times_state_t(v[:, cols(h)], suffix)).astype(BF16)
         gvb[:, cols(h)] = (acc2[:, cols(h)] + times_state(k[:, cols(h)], suffix)).astype(BF16)
 
-    @pl.loop(0, half)
-    def _(i):
+    def backward_blocks(i):
         for h in (mine(i), other(i)):
             at = cols(h)
             for held, (lo, hi) in zip((probs_a, probs_b), early):
@@ -273,6 +286,16 @@
                 d_probs = masked(dot(g[lo:hi, at], v[:hi, at], 1, 1), lo)
                 grad_q = dot(d_probs, k[:hi, at], 1, 0) + times_state_t(g[lo:hi, at], pre[h])
                 gqb[lo:hi, at] = grad_q.astype(BF16)
+
+    @pl.loop(0, ahead_down)
+    def _(i):
+        backward_blocks(i)
+
+    @pl.loop(0, half)
+    def _(i):
+        @pl.when(i + ahead_down < half)
+        def _():
+            backward_blocks(i + ahead_down)
 
         finish(mine(i), down.step(i))
 

time: 101 us -> 102 us (level)
  no operation moved by 1% of the time
where the time goes in v4:
time: 102 us
  Pallas kernels  101 us (99%)
    pallas_call x1, Pallas kernels, local(): pl.pallas_call(functools.partial(kernel, S, D, T, H), out_shape=(held, he...  96.4 us
    pallas_call x1, Pallas kernels, local(): pl.pallas_call(write, out_shape=(big,) * 4 + (jax.ShapeDtypeStruct((H, HD...  4.73 us

profile of v4, /device:TPU:1, one launch (start us, length us, event | category | flops | bytes accessed | tf_op | source)
XLA Modules:
  0.0 101.8 jit_solution(14898758875664079876)
XLA Ops:
  0.6 96.4 %shard_map.92 = (bf16[384,4096]{1,0:T(8,128)(2,1)S(1)}, bf16[384,4096]{1,0:T(8,128)(2,1)S(1)}, bf16[384,4096]{1,0:T(8,128)(2,1)S(1)}, bf16[384,4096]{1,0:T(8,128)(2,1)S(1)}, f32[32,128]{1,0:T(8,128)S(1)}) custom-call(bf16[1,384,4096]{2,1,0:T(8,128)(2,1)} %q_hbm.1, bf16[1,384,4096]{2,1,0:T(8,128)(2,1)} %k_hbm.1, bf16[1,384,4096]{2,1,0:T(8,128)(2,1)} %v_hbm.1, ...), custom_call_target="tpu_custom_call" | custom-call | flops 10468982784 | bytes 25165824 | tf_op jit(solution)/shard_map/pallas_call | solution.py:361
  97.0 4.7 %shard_map.93 = (bf16[1,384,4096]{2,1,0:T(8,128)(2,1)}, bf16[1,384,4096]{2,1,0:T(8,128)(2,1)}, bf16[1,384,4096]{2,1,0:T(8,128)(2,1)}, bf16[1,384,4096]{2,1,0:T(8,128)(2,1)}, f32[32,128]{1,0:T(8,128)}) custom-call(bf16[384,4096]{1,0:T(8,128)(2,1)S(1)} %get-tuple-element.15.refs_0_, bf16[384,4096]{1,0:T(8,128)(2,1)S(1)} %get-tuple-element.16.refs_1_, ...), custom_call_target="tpu_custom_call" | custom-call | bytes 12582912 | tf_op jit(solution)/shard_map/pallas_call | solution.py:380
